TPU v7x, 32 devices: a whole 2x2x4 slice. The times are simulated.
32 devices in a mesh: orb: 8 (over y, x, core), probe: 4 (over z).
Axes of the slice: x: 2, y: 2, z: 4, core: 2. Of those that a mesh axis runs over, the one named last changes fastest.
Arguments:
- tiles: bfloat16 [32, 9, 256, 256], P('orb', None, 'probe'), may hold values from -0.0625 to 0.0625
- pattern: int32 [32, 9], P('orb'), may hold values from 0 to 1, as said below
- signs: int32 [8192, 512], P('orb', 'probe'), may hold values from 0 to 1
- previous: bfloat16 [8192, 512], P('orb', 'probe'), may hold values from -6 to 6
- current: bfloat16 [8192, 512], P('orb', 'probe'), may hold values from -6 to 6
Outputs:
- older: bfloat16 [8192, 512], P('orb', 'probe')
- newest: bfloat16 [8192, 512], P('orb', 'probe')
- moments: float32 [4, 512], P(None, 'probe')
Inputs may be any that keep to these rules, and one draw needn't show every extreme that they name: pattern[I, 4] is 1 for every row block; each row block has 4 to 9 ones; the 4 row blocks of one index of orb hold at most 28 ones together, and some index of orb holds exactly 28.
All inputs are finite; a program needn't handle non-finite values.
Results may differ from a plain program's by a relative error of at most 0.0053.
Values may be sent and summed in bfloat16 or wider, within the bound.
A program may use at most 64 MiB of HBM per device.

v0:
```python
import math
import jax
import jax.numpy as jnp
from jax import lax
from jax.sharding import PartitionSpec as P

REACH = 4
STEPS = 4


def extended(array, sides, width):
    for axis, dim in sides:
        peers, length = (lax.axis_size(axis), array.shape[dim])
        up = [(i, (i + 1) % peers) for i in range(peers)]
        down = [(j, i) for i, j in up]
        last = lax.slice_in_dim(array, length - width, length, axis=dim)
        initial = lax.slice_in_dim(array, 0, width, axis=dim)
        before = lax.ppermute(last, axis, up)
        after = lax.ppermute(initial, axis, down)
        array = jnp.concatenate([before, array, after], axis=dim)
    return array


def extend_panel(vec, block_rows):
    return extended(vec, (("orb", 0),), REACH * block_rows)


def body(tiles, pattern, signs, previous, current):
    row_blocks, offsets, shard_rows, block_rows = tiles.shape
    probe_count = previous.shape[1]
    sign_f = (2 * signs - 1).astype(jnp.float32)
    factor = 1.0 / math.sqrt(lax.axis_size("orb") * row_blocks * block_rows)
    full_tiles = lax.all_gather(tiles, "probe", axis=2, tiled=True)
    mask_b = pattern.astype(jnp.bfloat16)
    older, newest = (previous, current)
    collected = []
    for step in range(STEPS):
        blocks = extend_panel(newest, block_rows).reshape(
            row_blocks + 2 * REACH, block_rows, probe_count
        )
        windows = jnp.stack(
            [blocks[offset : offset + row_blocks] for offset in range(offsets)], axis=1
        )
        windows = windows * mask_b[:, :, None, None]
        total = jnp.einsum(
            "roij,rojp->rip", full_tiles, windows, preferred_element_type=jnp.float32
        )
        image = total.reshape(row_blocks * block_rows, probe_count)
        nxt = (2.0 * image - older.astype(jnp.float32)).astype(jnp.bfloat16)
        local_sum = jnp.sum(sign_f * nxt.astype(jnp.float32), axis=0)
        collected.append(lax.psum(local_sum, "orb") * factor)
        older, newest = (newest, nxt)
    stacked = jnp.stack(collected)
    return (older, newest, stacked)


def solution(mesh):
    placed = (
        P("orb", None, "probe", None),
        P("orb", None),
        P("orb", "probe"),
        P("orb", "probe"),
        P("orb", "probe"),
    )
    return jax.shard_map(
        body,
        mesh=mesh,
        in_specs=placed,
        out_specs=(P("orb", "probe"), P("orb", "probe"), P(None, "probe")),
        check_vma=False,
    )
```

profile of v0, /device:TPU:0, one launch (start us, length us, event | category | flops | bytes accessed | tf_op | source)
XLA Modules:
  0.0 224.4 jit_solution(14347151901448904519)
XLA Ops:
  8.4 2.9 %collective-permute-start.1 = (bf16[1024,128]{1,0:T(8,128)(2,1)}, bf16[1024,128]{1,0:T(8,128)(2,1)S(1)}, u32[]{:S(2)}, u32[]{:S(2)}) collective-permute-start(bf16[1024,128]{1,0:T(8,128)(2,1)} %param.9), channel_id=1, source_target_pairs={{4,0},{8,4},{12,8},{16,12},{20,16},{24,20},{28,24},{0,28},{5,1},{9... | collective-permute-start | bytes 786440 | tf_op jit(solution)/shard_map/ppermute | solution.py:19
  11.4 1.1 copy.48
  13.2 2.5 %collective-permute-done = bf16[1024,128]{1,0:T(8,128)(2,1)S(1)} collective-permute-done((bf16[1024,128]{1,0:T(8,128)(2,1)}, bf16[1024,128]{1,0:T(8,128)(2,1)S(1)}, u32[]{:S(2)}, u32[]{:S(2)}) %collective-permute-start) | collective-permute-done | bytes 262176 | tf_op jit(solution)/shard_map/ppermute | solution.py:18
  15.8 1.5 collective-permute-done.1
  23.0 1.1 constant_dynamic-update-slice_fusion.12
  24.1 1.0 constant_dynamic-update-slice_fusion.10
  25.3 76.4 %all-gather.2.cloned.1.call-done = bf16[4,9,256,256]{3,2,1,0:T(8,128)(2,1)} async-done(((bf16[4,9,64,256]{3,2,1,0:T(8,128)(2,1)}), bf16[4,9,256,256]{3,2,1,0:T(8,128)(2,1)}) %all-gather.2.cloned.1.call-update) | async-done | bytes 4718608 | tf_op jit(solution)/shard_map/all_gather | solution.py:33
  101.7 4.0 %fusion.41 = f32[4,256,128]{1,2,0:T(8,128)S(1)} fusion(bf16[4,9,256,256]{3,2,1,0:T(8,128)(2,1)} %all-gather.2.cloned.1.call-done, bf16[4,9,256,128]{2,3,1,0:T(8,128)(2,1)S(1)} %constant_dynamic-update-slice_fusion.4, bf16[4,9]{1,0:T(4,128)(2,1)S(1)} %convert_element_type.38), kind=kOutput, calls=%fused_computation.19 | convolution fusion | flops 605290496 | bytes 7602248 | tf_op jit(solution)/shard_map/roij,rojp->rip/dot_general | solution.py:45
  105.9 1.1 fusion.53
  107.0 2.6 %collective-permute-start.3 = (bf16[1024,128]{1,0:T(8,128)(2,1)S(1)}, bf16[1024,128]{1,0:T(8,128)(2,1)S(1)}, u32[]{:S(2)}, u32[]{:S(2)}) collective-permute-start(bf16[1024,128]{1,0:T(8,128)(2,1)S(1)} %fusion.53), channel_id=1, source_target_pairs={{4,0},{8,4},{12,8},{16,12},{20,16},{24,20},{28,24},{0,28},{5,1},{9... | collective-permute-start | bytes 786440 | tf_op jit(solution)/shard_map/ppermute | solution.py:19
  110.5 4.2 %collective-permute-done.2 = bf16[1024,128]{1,0:T(8,128)(2,1)S(1)} collective-permute-done((bf16[1024,128]{1,0:T(8,128)(2,1)S(1)}, bf16[1024,128]{1,0:T(8,128)(2,1)S(1)}, u32[]{:S(2)}, u32[]{:S(2)}) %collective-permute-start.2) | collective-permute-done | bytes 262176 | tf_op jit(solution)/shard_map/ppermute | solution.py:18
  114.7 1.0 pad_maximum_fusion.4
  118.4 1.8 copy.56
  120.2 1.8 copy.57
  122.0 1.8 copy.59
  123.8 1.8 copy.60
  126.6 1.0 constant_dynamic-update-slice_fusion.20
  127.7 1.0 constant_dynamic-update-slice_fusion.19
  129.6 1.0 constant_dynamic-update-slice_fusion.17
  130.6 1.0 constant_dynamic-update-slice_fusion.16
  131.7 4.0 %fusion.35 = f32[4,256,128]{1,2,0:T(8,128)S(1)} fusion(bf16[4,9,256,256]{3,2,1,0:T(8,128)(2,1)} %all-gather.2.cloned.1.call-done, bf16[4,9,256,128]{2,3,1,0:T(8,128)(2,1)S(1)} %constant_dynamic-update-slice_fusion.13, bf16[4,9]{1,0:T(4,128)(2,1)S(1)} %convert_element_type.38), kind=kOutput, calls=%fused_computation.17 | convolution fusion | flops 605290496 | bytes 7602248 | tf_op jit(solution)/shard_map/roij,rojp->rip/dot_general | solution.py:45
  135.9 1.7 collective-permute-start.4
  137.7 1.1 collective-permute-start.5
  139.6 4.7 %collective-permute-done.4 = bf16[1024,128]{1,0:T(8,128)(2,1)S(1)} collective-permute-done((bf16[1024,128]{1,0:T(8,128)(2,1)S(1)}, bf16[1024,128]{1,0:T(8,128)(2,1)S(1)}, u32[]{:S(2)}, u32[]{:S(2)}) %collective-permute-start.4) | collective-permute-done | bytes 262176 | tf_op jit(solution)/shard_map/ppermute | solution.py:18
  144.4 1.0 pad_maximum_fusion.2
  148.1 1.8 copy.66
  149.9 1.8 copy.67
  151.7 1.8 copy.69
  153.5 1.8 copy.70
  156.3 1.0 constant_dynamic-update-slice_fusion.29
  157.3 1.0 constant_dynamic-update-slice_fusion.28
  159.3 1.0 constant_dynamic-update-slice_fusion.26
  161.3 4.8 %fusion.29 = f32[4,256,128]{1,2,0:T(8,128)} fusion(bf16[4,9,256,256]{3,2,1,0:T(8,128)(2,1)} %all-gather.2.cloned.1.call-done, bf16[4,9,256,128]{2,3,1,0:T(8,128)(2,1)S(1)} %constant_dynamic-update-slice_fusion.22, bf16[4,9]{1,0:T(4,128)(2,1)S(1)} %convert_element_type.38), kind=kOutput, calls=%fused_computation.15 | convolution fusion | flops 605290496 | bytes 7602248 | tf_op jit(solution)/shard_map/roij,rojp->rip/dot_general | solution.py:45
  166.1 1.2 copy.73
  167.5 2.0 collective-permute-start.6
  171.0 5.2 %collective-permute-done.6 = bf16[1024,128]{1,0:T(8,128)(2,1)S(1)} collective-permute-done((bf16[1024,128]{1,0:T(8,128)(2,1)S(1)}, bf16[1024,128]{1,0:T(8,128)(2,1)S(1)}, u32[]{:S(2)}, u32[]{:S(2)}) %collective-permute-start.6) | collective-permute-done | bytes 262176 | tf_op jit(solution)/shard_map/ppermute | solution.py:18
  176.2 1.2 pad_maximum_fusion
  180.0 1.8 copy.76
  181.8 1.8 copy.77
  183.6 1.8 copy.79
  185.4 1.8 copy.80
  187.2 1.8 copy.81
  189.9 1.0 constant_dynamic-update-slice_fusion.38
  190.9 1.0 constant_dynamic-update-slice_fusion.37
  194.9 4.8 %fusion.23 = f32[4,256,128]{1,2,0:T(8,128)} fusion(bf16[4,9,256,256]{3,2,1,0:T(8,128)(2,1)} %all-gather.2.cloned.1.call-done, bf16[4,9,256,128]{2,3,1,0:T(8,128)(2,1)S(1)} %constant_dynamic-update-slice_fusion.31, bf16[4,9]{1,0:T(4,128)(2,1)S(1)} %convert_element_type.38), kind=kOutput, calls=%fused_computation.13 | convolution fusion | flops 605290496 | bytes 7602248 | tf_op jit(solution)/shard_map/roij,rojp->rip/dot_general | solution.py:45
  199.7 1.2 copy.83
  201.0 2.0 fusion.49
  203.0 13.9 %all-reduce = (f32[128]{0:T(128)S(1)}, f32[128]{0:T(128)S(1)}, f32[128]{0:T(128)S(1)}, f32[128]{0:T(128)S(1)}) all-reduce(f32[128]{0:T(128)S(1)} %get-tuple-element.4, f32[128]{0:T(128)S(1)} %get-tuple-element.5, f32[128]{0:T(128)S(1)} %get-tuple-element.6, f32[128]{0:T(128)S(1)} %get-tuple-element.3), channel_id=1, replica_groups=mesh['orb'=8,'probe'=4] {'orb'}, use_global_device_ids=true, to_apply=%region_7.0 | all-reduce | flops 512 | bytes 4096 | tf_op jit(solution)/shard_map/psum | solution.py:51
  (95 shorter events, 29.1 us)
Async XLA Ops:
  7.2 8.6 %copy-start.1 = (bf16[1024,128]{1,0:T(8,128)(2,1)S(1)}, bf16[1024,128]{1,0:T(8,128)(2,1)}, u32[]{:S(2)}) copy-start(bf16[1024,128]{1,0:T(8,128)(2,1)} %param.9) | copy-start | bytes 786436
  7.2 94.5 %all-gather.2.cloned.1.call-start = ((), (), s32[]{:S(2)}) async-start(), calls=%async_computation | async-start | bytes 5898240 | tf_op jit(solution)/shard_map/all_gather | solution.py:33
  7.9 7.8 %collective-permute-start = (bf16[1024,128]{1,0:T(8,128)(2,1)}, bf16[1024,128]{1,0:T(8,128)(2,1)S(1)}, u32[]{:S(2)}, u32[]{:S(2)}) collective-permute-start(bf16[1024,128]{1,0:T(8,128)(2,1)} %param.9), channel_id=1, source_target_pairs={{0,4},{4,8},{8,12},{12,16},{16,20},{20,24},{24,28},{28,0},{1,5},{5... | collective-permute-start | bytes 786440 | tf_op jit(solution)/shard_map/ppermute | solution.py:18
  8.4 8.9 %collective-permute-start.1 = (bf16[1024,128]{1,0:T(8,128)(2,1)}, bf16[1024,128]{1,0:T(8,128)(2,1)S(1)}, u32[]{:S(2)}, u32[]{:S(2)}) collective-permute-start(bf16[1024,128]{1,0:T(8,128)(2,1)} %param.9), channel_id=1, source_target_pairs={{4,0},{8,4},{12,8},{16,12},{20,16},{24,20},{28,24},{0,28},{5,1},{9... | collective-permute-start | bytes 786440 | tf_op jit(solution)/shard_map/ppermute | solution.py:19
  23.0 2.1 copy-start.5
  23.0 2.2 copy-start.3
  23.0 2.2 copy-start.4
  23.0 2.2 copy-start.2
  107.0 7.7 %collective-permute-start.2 = (bf16[1024,128]{1,0:T(8,128)(2,1)S(1)}, bf16[1024,128]{1,0:T(8,128)(2,1)S(1)}, u32[]{:S(2)}, u32[]{:S(2)}) collective-permute-start(bf16[1024,128]{1,0:T(8,128)(2,1)S(1)} %fusion.53), channel_id=1, source_target_pairs={{0,4},{4,8},{8,12},{12,16},{16,20},{20,24},{24,28},{28,0},{1,5},{5... | collective-permute-start | bytes 786440 | tf_op jit(solution)/shard_map/ppermute | solution.py:18
  107.0 7.7 %collective-permute-start.3 = (bf16[1024,128]{1,0:T(8,128)(2,1)S(1)}, bf16[1024,128]{1,0:T(8,128)(2,1)S(1)}, u32[]{:S(2)}, u32[]{:S(2)}) collective-permute-start(bf16[1024,128]{1,0:T(8,128)(2,1)S(1)} %fusion.53), channel_id=1, source_target_pairs={{4,0},{8,4},{12,8},{16,12},{20,16},{24,20},{28,24},{0,28},{5,1},{9... | collective-permute-start | bytes 786440 | tf_op jit(solution)/shard_map/ppermute | solution.py:19
  126.6 4.9 %copy-start.7 = (bf16[4,1,256,128]{2,3,1,0:T(8,128)(2,1)S(1)}, bf16[4,1,256,128]{2,3,1,0:T(8,128)(2,1)}, u32[]{:S(2)}) copy-start(bf16[4,1,256,128]{2,3,1,0:T(8,128)(2,1)} %copy.60) | copy-start | bytes 786436
  126.6 5.0 %copy-start.8 = (bf16[4,1,256,128]{2,3,1,0:T(8,128)(2,1)S(1)}, bf16[4,1,256,128]{2,3,1,0:T(8,128)(2,1)}, u32[]{:S(2)}) copy-start(bf16[4,1,256,128]{2,3,1,0:T(8,128)(2,1)} %copy.61) | copy-start | bytes 786436
  135.9 8.4 %collective-permute-start.4 = (bf16[1024,128]{1,0:T(8,128)(2,1)S(1)}, bf16[1024,128]{1,0:T(8,128)(2,1)S(1)}, u32[]{:S(2)}, u32[]{:S(2)}) collective-permute-start(bf16[1024,128]{1,0:T(8,128)(2,1)S(1)} %fusion.52), channel_id=1, source_target_pairs={{0,4},{4,8},{8,12},{12,16},{16,20},{20,24},{24,28},{28,0},{1,5},{5... | collective-permute-start | bytes 786440 | tf_op jit(solution)/shard_map/ppermute | solution.py:18
  137.7 6.7 %collective-permute-start.5 = (bf16[1024,128]{1,0:T(8,128)(2,1)S(1)}, bf16[1024,128]{1,0:T(8,128)(2,1)S(1)}, u32[]{:S(2)}, u32[]{:S(2)}) collective-permute-start(bf16[1024,128]{1,0:T(8,128)(2,1)S(1)} %fusion.52), channel_id=1, source_target_pairs={{4,0},{8,4},{12,8},{16,12},{20,16},{24,20},{28,24},{0,28},{5,1},{9... | collective-permute-start | bytes 786440 | tf_op jit(solution)/shard_map/ppermute | solution.py:19
  156.3 4.9 %copy-start.9 = (bf16[4,1,256,128]{2,3,1,0:T(8,128)(2,1)S(1)}, bf16[4,1,256,128]{2,3,1,0:T(8,128)(2,1)}, u32[]{:S(2)}) copy-start(bf16[4,1,256,128]{2,3,1,0:T(8,128)(2,1)} %copy.70) | copy-start | bytes 786436
  156.3 5.0 %copy-start.10 = (bf16[4,1,256,128]{2,3,1,0:T(8,128)(2,1)S(1)}, bf16[4,1,256,128]{2,3,1,0:T(8,128)(2,1)}, u32[]{:S(2)}) copy-start(bf16[4,1,256,128]{2,3,1,0:T(8,128)(2,1)} %copy.71) | copy-start | bytes 786436
  167.4 33.5 %copy-start = (bf16[1024,128]{1,0:T(8,128)(2,1)}, bf16[1024,128]{1,0:T(8,128)(2,1)S(1)}, u32[]{:S(2)}) copy-start(bf16[1024,128]{1,0:T(8,128)(2,1)S(1)} %fusion.48) | copy-start | bytes 786436
  167.5 8.7 %collective-permute-start.6 = (bf16[1024,128]{1,0:T(8,128)(2,1)S(1)}, bf16[1024,128]{1,0:T(8,128)(2,1)S(1)}, u32[]{:S(2)}, u32[]{:S(2)}) collective-permute-start(bf16[1024,128]{1,0:T(8,128)(2,1)S(1)} %fusion.48), channel_id=1, source_target_pairs={{0,4},{4,8},{8,12},{12,16},{16,20},{20,24},{24,28},{28,0},{1,5},{5... | collective-permute-start | bytes 786440 | tf_op jit(solution)/shard_map/ppermute | solution.py:18
  169.5 6.7 %collective-permute-start.7 = (bf16[1024,128]{1,0:T(8,128)(2,1)S(1)}, bf16[1024,128]{1,0:T(8,128)(2,1)S(1)}, u32[]{:S(2)}, u32[]{:S(2)}) collective-permute-start(bf16[1024,128]{1,0:T(8,128)(2,1)S(1)} %fusion.48), channel_id=1, source_target_pairs={{4,0},{8,4},{12,8},{16,12},{20,16},{24,20},{28,24},{0,28},{5,1},{9... | collective-permute-start | bytes 786440 | tf_op jit(solution)/shard_map/ppermute | solution.py:19
  189.9 4.9 %copy-start.11 = (bf16[4,1,256,128]{2,3,1,0:T(8,128)(2,1)S(1)}, bf16[4,1,256,128]{2,3,1,0:T(8,128)(2,1)}, u32[]{:S(2)}) copy-start(bf16[4,1,256,128]{2,3,1,0:T(8,128)(2,1)} %copy.80) | copy-start | bytes 786436
  189.9 5.0 %copy-start.12 = (bf16[4,1,256,128]{2,3,1,0:T(8,128)(2,1)S(1)}, bf16[4,1,256,128]{2,3,1,0:T(8,128)(2,1)}, u32[]{:S(2)}) copy-start(bf16[4,1,256,128]{2,3,1,0:T(8,128)(2,1)} %copy.81) | copy-start | bytes 786436
  189.9 5.0 %copy-start.6 = (bf16[4,1,256,128]{2,3,1,0:T(8,128)(2,1)S(1)}, bf16[4,1,256,128]{2,3,1,0:T(8,128)(2,1)}, u32[]{:S(2)}) copy-start(bf16[4,1,256,128]{2,3,1,0:T(8,128)(2,1)} %copy.82) | copy-start | bytes 786436
Sparse Core Ops, SparseCore 0:
  9.6 92.0 all-gather.1
where the time goes:
time: 226 us; the launch traced here: 224 us
  waiting for transfers between devices  95.2 us (42%)
  local copies, waits for them, and re-layouts  63.6 us (28%)
  matrix products  17.6 us (8%)
  between operations  14.6 us (6%)
  blocking collectives  13.9 us (6%)
  starting transfers between devices  11.7 us (5%)
  other arithmetic  7.73 us (3%)
    all_gather x1, waiting for transfers between devices, body(): full_tiles = lax.all_gather(tiles, 'probe', axis=2, tiled=True)  76.4 us
    another operation x40, local copies, waits for them, and re-layouts, body(): jnp.stack([blocks[offset:offset + row_blocks] for offset in range(offsets...  40.6 us
    unnamed x60, local copies, waits for them, and re-layouts  20 us
    dot_general x4, matrix products, body(): jnp.einsum('roij,rojp->rip', full_tiles, windows, preferred_element_type=...  17.6 us
    ppermute x4, waiting for transfers between devices, extended(): before = lax.ppermute(last, axis, up)  16.6 us
    psum x1, blocking collectives, body(): collected.append(lax.psum(local_sum, 'orb') * factor)  13.9 us
    ppermute x4, starting transfers between devices, extended(): after = lax.ppermute(initial, axis, down)  7.37 us
  transfers between devices with their start and end apart: 9, of which 6 were waited for; matrix products, arithmetic and copies ran while one was open for 5% of the time, Pallas kernels for 0%

commit v1 on v0

--- a/solution.py
+++ b/solution.py
@@ -30,7 +30,14 @@
     probe_count = previous.shape[1]
     sign_f = (2 * signs - 1).astype(jnp.float32)
     factor = 1.0 / math.sqrt(lax.axis_size("orb") * row_blocks * block_rows)
-    full_tiles = lax.all_gather(tiles, "probe", axis=2, tiled=True)
+    ring = [tiles]
+    for hop in range(3):
+        ring.append(lax.ppermute(ring[-1], "probe", [(dev, (dev + 1) % 4) for dev in range(4)]))
+    full_tiles = jnp.roll(
+        jnp.concatenate(ring[::-1], axis=2),
+        (lax.axis_index("probe") + 1) * ring[0].shape[2],
+        axis=2,
+    )
     mask_b = pattern.astype(jnp.bfloat16)
     older, newest = (previous, current)
     collected = []

time: 226 us -> 139 us (0.62)
  local copies, waits for them, and re-layouts: 63.6 us -> 4.42 us
  between operations: 14.6 us -> 1.16 us
  matrix products: 17.6 us -> 5.82 us
  other arithmetic: 7.73 us -> 3.02 us
  waiting for transfers between devices: 95.2 us -> 98.7 us
    all_gather x1 -> x0, waiting for transfers between devices: 76.4 us -> none  [body(): full_tiles = lax.all_gather(tiles, 'probe', axis=2, tiled=True)]
    ppermute x0 -> x3, waiting for transfers between devices: none -> 75.6 us  [body(): lax.ppermute(ring[-1], 'probe', [(dev, (dev + 1) % 4) for dev in range(4)])]
    another operation x40 -> x4, local copies, waits for them, and re-layouts: 40.6 us -> 0.15 us  [body(): jnp.stack([blocks[offset:offset + row_blocks] for offset in range(offsets...]
    unnamed x60 -> x51, local copies, waits for them, and re-layouts: 20 us -> 3.97 us
    dot_general x4, matrix products: 17.6 us -> 5.82 us  [body(): jnp.einsum('roij,rojp->rip', full_tiles, windows, preferred_element_type=...]
    ppermute x4, waiting for transfers between devices: 16.6 us -> 23.1 us  [extended(): before = lax.ppermute(last, axis, up)]
    ppermute x0 -> x3, starting transfers between devices: none -> 3.08 us  [body(): lax.ppermute(ring[-1], 'probe', [(dev, (dev + 1) % 4) for dev in range(4)])]
    ppermute x4, starting transfers between devices: 4.31 us -> 1.27 us  [extended(): before = lax.ppermute(last, axis, up)]
  transfers between devices with their start and end apart: 9 -> 11, of which waited for: 6 -> 7; matrix products, arithmetic and copies ran while one was open for 5% -> 2% of each run, Pallas kernels for 0% -> 0%
where the time goes in v1:
time: 139 us
  waiting for transfers between devices  98.7 us (71%)
  starting transfers between devices  13.8 us (10%)
  blocking collectives  11.8 us (8%)
  matrix products  5.82 us (4%)
  local copies, waits for them, and re-layouts  4.42 us (3%)
  other arithmetic  3.02 us (2%)
    ppermute x3, waiting for transfers between devices, body(): lax.ppermute(ring[-1], 'probe', [(dev, (dev + 1) % 4) for dev in range(4)])  75.6 us
    ppermute x4, waiting for transfers between devices, extended(): before = lax.ppermute(last, axis, up)  23.1 us
    psum x1, blocking collectives, body(): collected.append(lax.psum(local_sum, 'orb') * factor)  11.8 us
    ppermute x4, starting transfers between devices, extended(): after = lax.ppermute(initial, axis, down)  9.46 us
    dot_general x4, matrix products, body(): jnp.einsum('roij,rojp->rip', full_tiles, windows, preferred_element_type=...  5.82 us
    unnamed x51, local copies, waits for them, and re-layouts  3.97 us
    ppermute x3, starting transfers between devices, body(): lax.ppermute(ring[-1], 'probe', [(dev, (dev + 1) % 4) for dev in range(4)])  3.08 us
  transfers between devices with their start and end apart: 11, of which 7 were waited for; matrix products, arithmetic and copies ran while one was open for 2% of the time, Pallas kernels for 0%

profile of v1, /device:TPU:0, one launch (start us, length us, event | category | flops | bytes accessed | tf_op | source)
XLA Modules:
  0.0 138.7 jit_solution(6313543482221781230)
XLA Ops:
  0.6 3.1 %collective-permute-start = (bf16[4,9,64,256]{3,2,1,0:T(8,128)(2,1)}, bf16[4,9,64,256]{3,2,1,0:T(8,128)(2,1)S(1)}, u32[]{:S(2)}, u32[]{:S(2)}) collective-permute-start(bf16[4,9,64,256]{3,2,1,0:T(8,128)(2,1)} %param.5), channel_id=1, source_target_pairs={{0,1},{1,2},{2,3},{3,0},{4,5},{5,6},{6,7},{7,4},{8,9},{9,10},{10,1... | collective-permute-start | bytes 3538952 | tf_op jit(solution)/shard_map/ppermute | solution.py:35
  3.7 28.2 %collective-permute-done = bf16[4,9,64,256]{3,2,1,0:T(8,128)(2,1)S(1)} collective-permute-done((bf16[4,9,64,256]{3,2,1,0:T(8,128)(2,1)}, bf16[4,9,64,256]{3,2,1,0:T(8,128)(2,1)S(1)}, u32[]{:S(2)}, u32[]{:S(2)}) %collective-permute-start) | collective-permute-done | bytes 1179680 | tf_op jit(solution)/shard_map/ppermute | solution.py:35
  31.9 0.0 collective-permute-start.1
  31.9 0.0 collective-permute-start.3
  31.9 2.6 %collective-permute-start.4 = (bf16[1024,128]{1,0:T(8,128)(2,1)}, bf16[1024,128]{1,0:T(8,128)(2,1)S(1)}, u32[]{:S(2)}, u32[]{:S(2)}) collective-permute-start(bf16[1024,128]{1,0:T(8,128)(2,1)} %param.9), channel_id=1, source_target_pairs={{4,0},{8,4},{12,8},{16,12},{20,16},{24,20},{28,24},{0,28},{5,1},{9... | collective-permute-start | bytes 786440 | tf_op jit(solution)/shard_map/ppermute | solution.py:19
  34.6 0.7 convert_element_type.38
  35.2 4.5 %collective-permute-done.3 = bf16[1024,128]{1,0:T(8,128)(2,1)S(1)} collective-permute-done((bf16[1024,128]{1,0:T(8,128)(2,1)}, bf16[1024,128]{1,0:T(8,128)(2,1)S(1)}, u32[]{:S(2)}, u32[]{:S(2)}) %collective-permute-start.3) | collective-permute-done | bytes 262176 | tf_op jit(solution)/shard_map/ppermute | solution.py:18
  39.8 0.0 copy-start.2
  39.8 1.1 constant_dynamic-update-slice_fusion.11
  40.9 0.1 fusion.80
  41.0 19.8 %collective-permute-done.1 = bf16[4,9,64,256]{3,2,1,0:T(8,128)(2,1)S(1)} collective-permute-done((bf16[4,9,64,256]{3,2,1,0:T(8,128)(2,1)S(1)}, bf16[4,9,64,256]{3,2,1,0:T(8,128)(2,1)S(1)}, u32[]{:S(2)}, u32[]{:S(2)}) %collective-permute-start.1) | collective-permute-done | bytes 1179680 | tf_op jit(solution)/shard_map/ppermute | solution.py:35
  61.0 0.1 fusion.79
  61.3 27.6 %collective-permute-done.2 = bf16[4,9,64,256]{3,2,1,0:T(8,128)(2,1)S(1)} collective-permute-done((bf16[4,9,64,256]{3,2,1,0:T(8,128)(2,1)S(1)}, bf16[4,9,64,256]{3,2,1,0:T(8,128)(2,1)S(1)}, u32[]{:S(2)}, u32[]{:S(2)}) %collective-permute-start.2) | collective-permute-done | bytes 1179680 | tf_op jit(solution)/shard_map/ppermute | solution.py:35
  88.9 0.1 constant_dynamic-update-slice_fusion.7
  89.0 0.0 copy-start
  89.0 0.1 constant_dynamic-update-slice_fusion.6
  89.1 0.1 constant_dynamic-update-slice_fusion.5
  89.2 1.0 copy-done
  90.3 0.1 constant_dynamic-update-slice_fusion.4
  90.3 0.1 constant_dynamic-update-slice_fusion.3
  90.4 0.1 constant_dynamic-update-slice_fusion.2
  90.5 0.1 constant_dynamic-update-slice_fusion.1
  90.7 0.1 constant_dynamic-update-slice_fusion
  90.8 0.0 copy-start.4
  90.8 1.5 %fusion.47 = f32[4,256,128]{2,1,0:T(8,128)S(1)} fusion(bf16[4,9,256,128]{3,2,1,0:T(8,128)(2,1)S(1)} %constant_dynamic-update-slice_fusion.12, bf16[4,9,512,256]{3,2,1,0:T(8,128)(2,1)S(1)} %constant_dynamic-update-slice_fusion, s32[]{:T(128)S(6)} %select_n.14, bf16[4,9]{1,0:T(4,128)(2,1)S(1)} %convert_element_type.38), kind=kOutput, calls=%fused_computation.19 | convolution fusion | flops 605290496 | bytes 7603204 | tf_op jit(solution)/shard_map/roij,rojp->rip/dot_general | solution.py:52
  92.2 0.1 fusion.61
  92.3 0.1 collective-permute-start.5
  92.4 2.6 %collective-permute-start.6 = (bf16[1024,128]{1,0:T(8,128)(2,1)S(1)}, bf16[1024,128]{1,0:T(8,128)(2,1)S(1)}, u32[]{:S(2)}, u32[]{:S(2)}) collective-permute-start(bf16[1024,128]{1,0:T(8,128)(2,1)S(1)} %fusion.61), channel_id=1, source_target_pairs={{4,0},{8,4},{12,8},{16,12},{20,16},{24,20},{28,24},{0,28},{5,1},{9... | collective-permute-start | bytes 786440 | tf_op jit(solution)/shard_map/ppermute | solution.py:19
  95.0 5.4 %collective-permute-done.5 = bf16[1024,128]{1,0:T(8,128)(2,1)S(1)} collective-permute-done((bf16[1024,128]{1,0:T(8,128)(2,1)S(1)}, bf16[1024,128]{1,0:T(8,128)(2,1)S(1)}, u32[]{:S(2)}, u32[]{:S(2)}) %collective-permute-start.5) | collective-permute-done | bytes 262176 | tf_op jit(solution)/shard_map/ppermute | solution.py:18
  100.5 0.2 pad_maximum_fusion.4
  101.0 1.5 %fusion.42 = f32[4,256,128]{2,1,0:T(8,128)S(1)} fusion(bf16[4,9,256,128]{3,2,1,0:T(8,128)(2,1)S(1)} %constant_dynamic-update-slice_fusion.21, bf16[4,9,512,256]{3,2,1,0:T(8,128)(2,1)S(1)} %constant_dynamic-update-slice_fusion, s32[]{:T(128)S(6)} %select_n.14, bf16[4,9]{1,0:T(4,128)(2,1)S(1)} %convert_element_type.38), kind=kOutput, calls=%fused_computation.18 | convolution fusion | flops 605290496 | bytes 7603204 | tf_op jit(solution)/shard_map/roij,rojp->rip/dot_general | solution.py:52
  102.5 0.1 fusion.60
  102.6 0.8 collective-permute-start.7
  103.4 1.9 %collective-permute-start.8 = (bf16[1024,128]{1,0:T(8,128)(2,1)S(1)}, bf16[1024,128]{1,0:T(8,128)(2,1)S(1)}, u32[]{:S(2)}, u32[]{:S(2)}) collective-permute-start(bf16[1024,128]{1,0:T(8,128)(2,1)S(1)} %fusion.60), channel_id=1, source_target_pairs={{4,0},{8,4},{12,8},{16,12},{20,16},{24,20},{28,24},{0,28},{5,1},{9... | collective-permute-start | bytes 786440 | tf_op jit(solution)/shard_map/ppermute | solution.py:19
  105.3 6.4 %collective-permute-done.7 = bf16[1024,128]{1,0:T(8,128)(2,1)S(1)} collective-permute-done((bf16[1024,128]{1,0:T(8,128)(2,1)S(1)}, bf16[1024,128]{1,0:T(8,128)(2,1)S(1)}, u32[]{:S(2)}, u32[]{:S(2)}) %collective-permute-start.7) | collective-permute-done | bytes 262176 | tf_op jit(solution)/shard_map/ppermute | solution.py:18
  111.7 0.2 pad_maximum_fusion.2
  112.2 1.5 %fusion.37 = f32[4,256,128]{2,1,0:T(8,128)S(1)} fusion(bf16[4,9,256,128]{3,2,1,0:T(8,128)(2,1)S(1)} %constant_dynamic-update-slice_fusion.30, bf16[4,9,512,256]{3,2,1,0:T(8,128)(2,1)S(1)} %constant_dynamic-update-slice_fusion, s32[]{:T(128)S(6)} %select_n.14, bf16[4,9]{1,0:T(4,128)(2,1)S(1)} %convert_element_type.38), kind=kOutput, calls=%fused_computation.17 | convolution fusion | flops 605290496 | bytes 7603204 | tf_op jit(solution)/shard_map/roij,rojp->rip/dot_general | solution.py:52
  113.7 0.1 fusion.56
  113.7 0.0 copy-start.1
  113.8 0.4 collective-permute-start.9
  114.1 2.3 %collective-permute-start.10 = (bf16[1024,128]{1,0:T(8,128)(2,1)S(1)}, bf16[1024,128]{1,0:T(8,128)(2,1)S(1)}, u32[]{:S(2)}, u32[]{:S(2)}) collective-permute-start(bf16[1024,128]{1,0:T(8,128)(2,1)S(1)} %fusion.56), channel_id=1, source_target_pairs={{4,0},{8,4},{12,8},{16,12},{20,16},{24,20},{28,24},{0,28},{5,1},{9... | collective-permute-start | bytes 786440 | tf_op jit(solution)/shard_map/ppermute | solution.py:19
  116.4 6.8 %collective-permute-done.9 = bf16[1024,128]{1,0:T(8,128)(2,1)S(1)} collective-permute-done((bf16[1024,128]{1,0:T(8,128)(2,1)S(1)}, bf16[1024,128]{1,0:T(8,128)(2,1)S(1)}, u32[]{:S(2)}, u32[]{:S(2)}) %collective-permute-start.9) | collective-permute-done | bytes 262176 | tf_op jit(solution)/shard_map/ppermute | solution.py:18
  123.2 0.2 pad_maximum_fusion
  123.8 0.0 copy-start.3
  123.8 1.5 %fusion.32 = f32[4,256,128]{2,1,0:T(8,128)S(1)} fusion(bf16[4,9,256,128]{3,2,1,0:T(8,128)(2,1)S(1)} %constant_dynamic-update-slice_fusion.39, bf16[4,9,512,256]{3,2,1,0:T(8,128)(2,1)S(1)} %constant_dynamic-update-slice_fusion, s32[]{:T(128)S(6)} %select_n.14, bf16[4,9]{1,0:T(4,128)(2,1)S(1)} %convert_element_type.38), kind=kOutput, calls=%fused_computation.16 | convolution fusion | flops 605290496 | bytes 7603204 | tf_op jit(solution)/shard_map/roij,rojp->rip/dot_general | solution.py:52
  125.3 1.0 fusion.57
  126.3 11.8 %all-reduce = (f32[128]{0:T(128)S(1)}, f32[128]{0:T(128)S(1)}, f32[128]{0:T(128)S(1)}, f32[128]{0:T(128)S(1)}) all-reduce(f32[128]{0:T(128)S(1)} %get-tuple-element.4, f32[128]{0:T(128)S(1)} %get-tuple-element.5, f32[128]{0:T(128)S(1)} %get-tuple-element.6, f32[128]{0:T(128)S(1)} %get-tuple-element.3), channel_id=1, replica_groups=mesh['orb'=8,'probe'=4] {'orb'}, use_global_device_ids=true, to_apply=%region_7.8 | all-reduce | flops 512 | bytes 4096 | tf_op jit(solution)/shard_map/psum | solution.py:58
  138.1 0.6 pad_maximum_fusion.6
  (50 shorter events, 1.3 us)
Async XLA Ops:
  0.6 31.3 %collective-permute-start = (bf16[4,9,64,256]{3,2,1,0:T(8,128)(2,1)}, bf16[4,9,64,256]{3,2,1,0:T(8,128)(2,1)S(1)}, u32[]{:S(2)}, u32[]{:S(2)}) collective-permute-start(bf16[4,9,64,256]{3,2,1,0:T(8,128)(2,1)} %param.5), channel_id=1, source_target_pairs={{0,1},{1,2},{2,3},{3,0},{4,5},{5,6},{6,7},{7,4},{8,9},{9,10},{10,1... | collective-permute-start | bytes 3538952 | tf_op jit(solution)/shard_map/ppermute | solution.py:35
  31.9 29.0 %collective-permute-start.1 = (bf16[4,9,64,256]{3,2,1,0:T(8,128)(2,1)S(1)}, bf16[4,9,64,256]{3,2,1,0:T(8,128)(2,1)S(1)}, u32[]{:S(2)}, u32[]{:S(2)}) collective-permute-start(bf16[4,9,64,256]{3,2,1,0:T(8,128)(2,1)S(1)} %collective-permute-done), channel_id=1, source_target_pairs={{0,1},{1,2},{2,3},{3,0},{4,5},{5,6},{6,7},{7,4},{8,9},{9,10},{10,1... | collective-permute-start | bytes 3538952 | tf_op jit(solution)/shard_map/ppermute | solution.py:35
  31.9 7.8 %collective-permute-start.3 = (bf16[1024,128]{1,0:T(8,128)(2,1)}, bf16[1024,128]{1,0:T(8,128)(2,1)S(1)}, u32[]{:S(2)}, u32[]{:S(2)}) collective-permute-start(bf16[1024,128]{1,0:T(8,128)(2,1)} %param.9), channel_id=1, source_target_pairs={{0,4},{4,8},{8,12},{12,16},{16,20},{20,24},{24,28},{28,0},{1,5},{5... | collective-permute-start | bytes 786440 | tf_op jit(solution)/shard_map/ppermute | solution.py:18
  31.9 9.0 %collective-permute-start.4 = (bf16[1024,128]{1,0:T(8,128)(2,1)}, bf16[1024,128]{1,0:T(8,128)(2,1)S(1)}, u32[]{:S(2)}, u32[]{:S(2)}) collective-permute-start(bf16[1024,128]{1,0:T(8,128)(2,1)} %param.9), channel_id=1, source_target_pairs={{4,0},{8,4},{12,8},{16,12},{20,16},{24,20},{28,24},{0,28},{5,1},{9... | collective-permute-start | bytes 786440 | tf_op jit(solution)/shard_map/ppermute | solution.py:19
  39.8 21.2 %copy-start.2 = (bf16[1024,128]{1,0:T(8,128)(2,1)S(1)}, bf16[1024,128]{1,0:T(8,128)(2,1)}, u32[]{:S(2)}) copy-start(bf16[1024,128]{1,0:T(8,128)(2,1)} %param.9) | copy-start | bytes 786436
  60.9 28.0 %collective-permute-start.2 = (bf16[4,9,64,256]{3,2,1,0:T(8,128)(2,1)S(1)}, bf16[4,9,64,256]{3,2,1,0:T(8,128)(2,1)S(1)}, u32[]{:S(2)}, u32[]{:S(2)}) collective-permute-start(bf16[4,9,64,256]{3,2,1,0:T(8,128)(2,1)S(1)} %collective-permute-done.1), channel_id=1, source_target_pairs={{0,1},{1,2},{2,3},{3,0},{4,5},{5,6},{6,7},{7,4},{8,9},{9,10},{10,1... | collective-permute-start | bytes 3538952 | tf_op jit(solution)/shard_map/ppermute | solution.py:35
  89.0 1.3 copy-start
  90.8 1.5 %copy-start.4 = (bf16[1024,128]{1,0:T(8,128)(2,1)S(1)}, bf16[1024,128]{1,0:T(8,128)(2,1)}, u32[]{:S(2)}) copy-start(bf16[1024,128]{1,0:T(8,128)(2,1)} %param.8) | copy-start | bytes 786436
  92.3 8.1 %collective-permute-start.5 = (bf16[1024,128]{1,0:T(8,128)(2,1)S(1)}, bf16[1024,128]{1,0:T(8,128)(2,1)S(1)}, u32[]{:S(2)}, u32[]{:S(2)}) collective-permute-start(bf16[1024,128]{1,0:T(8,128)(2,1)S(1)} %fusion.61), channel_id=1, source_target_pairs={{0,4},{4,8},{8,12},{12,16},{16,20},{20,24},{24,28},{28,0},{1,5},{5... | collective-permute-start | bytes 786440 | tf_op jit(solution)/shard_map/ppermute | solution.py:18
  92.4 8.1 %collective-permute-start.6 = (bf16[1024,128]{1,0:T(8,128)(2,1)S(1)}, bf16[1024,128]{1,0:T(8,128)(2,1)S(1)}, u32[]{:S(2)}, u32[]{:S(2)}) collective-permute-start(bf16[1024,128]{1,0:T(8,128)(2,1)S(1)} %fusion.61), channel_id=1, source_target_pairs={{4,0},{8,4},{12,8},{16,12},{20,16},{24,20},{28,24},{0,28},{5,1},{9... | collective-permute-start | bytes 786440 | tf_op jit(solution)/shard_map/ppermute | solution.py:19
  102.6 9.1 %collective-permute-start.7 = (bf16[1024,128]{1,0:T(8,128)(2,1)S(1)}, bf16[1024,128]{1,0:T(8,128)(2,1)S(1)}, u32[]{:S(2)}, u32[]{:S(2)}) collective-permute-start(bf16[1024,128]{1,0:T(8,128)(2,1)S(1)} %fusion.60), channel_id=1, source_target_pairs={{0,4},{4,8},{8,12},{12,16},{16,20},{20,24},{24,28},{28,0},{1,5},{5... | collective-permute-start | bytes 786440 | tf_op jit(solution)/shard_map/ppermute | solution.py:18
  103.4 8.3 %collective-permute-start.8 = (bf16[1024,128]{1,0:T(8,128)(2,1)S(1)}, bf16[1024,128]{1,0:T(8,128)(2,1)S(1)}, u32[]{:S(2)}, u32[]{:S(2)}) collective-permute-start(bf16[1024,128]{1,0:T(8,128)(2,1)S(1)} %fusion.60), channel_id=1, source_target_pairs={{4,0},{8,4},{12,8},{16,12},{20,16},{24,20},{28,24},{0,28},{5,1},{9... | collective-permute-start | bytes 786440 | tf_op jit(solution)/shard_map/ppermute | solution.py:19
  113.7 11.6 %copy-start.1 = (bf16[1024,128]{1,0:T(8,128)(2,1)}, bf16[1024,128]{1,0:T(8,128)(2,1)S(1)}, u32[]{:S(2)}) copy-start(bf16[1024,128]{1,0:T(8,128)(2,1)S(1)} %fusion.56) | copy-start | bytes 786436
  113.8 9.5 %collective-permute-start.9 = (bf16[1024,128]{1,0:T(8,128)(2,1)S(1)}, bf16[1024,128]{1,0:T(8,128)(2,1)S(1)}, u32[]{:S(2)}, u32[]{:S(2)}) collective-permute-start(bf16[1024,128]{1,0:T(8,128)(2,1)S(1)} %fusion.56), channel_id=1, source_target_pairs={{0,4},{4,8},{8,12},{12,16},{16,20},{20,24},{24,28},{28,0},{1,5},{5... | collective-permute-start | bytes 786440 | tf_op jit(solution)/shard_map/ppermute | solution.py:18
  114.1 9.1 %collective-permute-start.10 = (bf16[1024,128]{1,0:T(8,128)(2,1)S(1)}, bf16[1024,128]{1,0:T(8,128)(2,1)S(1)}, u32[]{:S(2)}, u32[]{:S(2)}) collective-permute-start(bf16[1024,128]{1,0:T(8,128)(2,1)S(1)} %fusion.56), channel_id=1, source_target_pairs={{4,0},{8,4},{12,8},{16,12},{20,16},{24,20},{28,24},{0,28},{5,1},{9... | collective-permute-start | bytes 786440 | tf_op jit(solution)/shard_map/ppermute | solution.py:19
  123.8 1.5 %copy-start.3 = (s32[1024,128]{1,0:T(8,128)S(1)}, s32[1024,128]{1,0:T(8,128)}, u32[]{:S(2)}) copy-start(s32[1024,128]{1,0:T(8,128)} %param.7) | copy-start | bytes 1572868
